TPU v7x, 32 devices: a whole 2x2x4 slice. The times are simulated.
32 devices in a mesh: groups: 2 (over x), seq: 16 (over z, y, core).
Axes of the slice: x: 2, y: 2, z: 4, core: 2. Of those that a mesh axis runs over, the one named last changes fastest.
Arguments:
- frames: bfloat16 [384, 256, 1280], P(('groups', 'seq')), parts along dimension 0, may hold values from -6 to 6
- match: int32 [384, 256], P(('groups', 'seq')), parts along dimension 0, may hold values from -1 to 255, as said below
- weight: int32 [384, 256], P(('groups', 'seq')), parts along dimension 0, may hold values from 1 to 8
- keep: int32 [384, 64], P(('groups', 'seq')), parts along dimension 0, may hold values from 0 to 1, as said below
- gain: float32 [1280], replicated, may hold values from 0.25 to 1.75
Outputs:
- merged_rows: bfloat16 [12288, 5120], P(('groups', 'seq')), parts along dimension 0
There are 2 independent parts, one for each index of `groups`. A program takes and returns all parts, laid end to end along the dimension named above; an argument that names none is the same for every part. Nothing has to cross between parts.
Inputs may be any that keep to these rules, and one draw needn't show every extreme that they name: `keep`: exactly 6144 groups are kept. Frame 0 keeps all its groups and every frame keeps one or more. For each i the kept groups of frames 0 to 12 * i - 1 number 384 * i plus or minus at most 180, and exactly 180 away for some i. match[f, t] is -1 where group t // 4 of frame f is kept, and otherwise names a token of frame f - 1 whose group is kept there.
All inputs are finite; a program needn't handle non-finite values.
Results may differ from a plain program's by a relative error of at most 0.0018.
Values may be sent and summed in bfloat16 or wider, within the bound.
A program may use at most 128 MiB of HBM per device.

v0:
```python
import jax
import jax.numpy as jnp
from jax import lax
from jax.sharding import PartitionSpec as P


def shifted(value, axis, steps):
    count = lax.axis_size(axis)
    leading, last = (max(0, -steps), min(count, count - steps))
    return lax.ppermute(value, axis, [(source, source + steps) for source in range(leading, last)])


def entering(shard, axis, combine, identity):
    length, position = (lax.axis_size(axis), lax.axis_index(axis))
    everything = lax.all_gather(shard, axis)
    start = jnp.broadcast_to(jnp.asarray(identity, shard.dtype), shard.shape)

    def turn(k, before):
        reached = k < position
        new = combine(before, everything[k])
        return jnp.where(reached, new, before)

    return lax.fori_loop(0, length, turn, start)


def absorb(source, targets, weights):
    slot_ids = jnp.arange(source.shape[1], dtype=jnp.int32)
    weighted = jnp.where(targets[:, None, :] == slot_ids[None, :, None], weights[:, None, :], 0)
    incoming = jnp.einsum(
        "fst,ftc->fsc", weighted.astype(jnp.bfloat16), source, preferred_element_type=jnp.float32
    )
    absorbed = jnp.sum(weighted, axis=2).astype(jnp.float32)
    return (incoming, absorbed)


def add_counts(earlier, later):
    return earlier + later


def body(frames, match, weight, keep, gain):
    count_frames = frames.shape[0]
    width = frames.shape[2]
    groups = keep.shape[1]
    kept_dev = count_frames * groups // 2
    drift_rows = kept_dev // 2 - count_frames
    position = lax.axis_index("seq")
    first_incoming, first_absorbed = absorb(frames[:1], match[:1], weight[:1])
    from_after, absorbed_after = (
        shifted(first_incoming[0].astype(jnp.bfloat16), "seq", -1).astype(jnp.float32),
        shifted(first_absorbed[0].astype(jnp.bfloat16), "seq", -1).astype(jnp.float32),
    )
    rest_incoming, rest_absorbed = absorb(frames[1:], match[1:], weight[1:])
    incoming = jnp.concatenate([rest_incoming, from_after[None]], axis=0)
    absorbed = jnp.concatenate([rest_absorbed, absorbed_after[None]], axis=0)
    own_weight = weight.astype(jnp.float32)
    merged = (own_weight[:, :, None] * frames.astype(jnp.float32) + incoming) / (
        own_weight + absorbed
    )[:, :, None]
    scale = lax.rsqrt(jnp.mean(merged * merged, axis=2, keepdims=True) + 1e-06)
    normed = (merged * scale * gain).astype(jnp.bfloat16)
    group_rows = normed.reshape(count_frames * groups, 4 * width)
    flat_keep = keep.reshape(-1)
    kept_count = jnp.sum(flat_keep)
    kept_start = entering(kept_count, "seq", add_counts, jnp.int32(0))
    offset = (position * kept_dev - kept_start).astype(jnp.int32)
    kept_order = jnp.argsort(1 - flat_keep, stable=True)
    compact = jnp.take(group_rows, kept_order, axis=0)
    live_rows = jnp.arange(compact.shape[0], dtype=jnp.int32) < kept_count
    compact = jnp.where(live_rows[:, None], compact, jnp.zeros_like(compact))
    blank_rows = jnp.zeros((kept_dev, 4 * width), jnp.bfloat16)
    padded = jnp.concatenate([blank_rows, compact, blank_rows], axis=0)
    own_rows = lax.dynamic_slice_in_dim(padded, offset + kept_dev, kept_dev, 0)
    to_next = lax.dynamic_slice_in_dim(padded, offset + 2 * kept_dev, drift_rows, 0)
    to_back = lax.dynamic_slice_in_dim(padded, offset + kept_dev - drift_rows, drift_rows, 0)
    tail_blank = jnp.zeros((kept_dev - drift_rows, 4 * width), jnp.bfloat16)
    from_next = shifted(to_next, "seq", 1)
    from_back = shifted(to_back, "seq", -1)
    result = own_rows + jnp.concatenate([from_next, tail_blank], axis=0)
    result = result + jnp.concatenate([tail_blank, from_back], axis=0)
    return result


def solution(mesh):
    placed = (
        P(("groups", "seq"), None, None),
        P(("groups", "seq"), None),
        P(("groups", "seq"), None),
        P(("groups", "seq"), None),
        P(),
    )
    return jax.shard_map(
        body, mesh=mesh, in_specs=placed, out_specs=P(("groups", "seq"), None), check_vma=False
    )
```

profile of v0, /device:TPU:1, one launch (start us, length us, event | category | flops | bytes accessed | tf_op | source)
XLA Modules:
  0.0 179.4 jit_solution(9059055576185713956)
XLA Ops:
  0.0 0.7 slice.21
  0.7 0.7 slice.22
  1.5 2.0 %collective-permute-start.1 = (bf16[256]{0:T(256)(128)(2,1)S(1)}, bf16[256]{0:T(256)(128)(2,1)S(1)}, u32[]{:S(2)}, u32[]{:S(2)}) collective-permute-start(bf16[256]{0:T(256)(128)(2,1)S(1)} %convert_convert_fusion), channel_id=1, source_target_pairs={{1,0},{2,1},{3,2},{4,3},{5,4},{6,5},{7,6},{8,7},{9,8},{10,9},{11,1... | collective-permute-start | bytes 1544 | tf_op jit(solution)/shard_map/ppermute | solution.py:10
  3.5 1.4 convolution_convert_fusion
  4.9 1.9 %collective-permute-start = (bf16[256,1280]{1,0:T(8,128)(2,1)S(1)}, bf16[256,1280]{1,0:T(8,128)(2,1)S(1)}, u32[]{:S(2)}, u32[]{:S(2)}) collective-permute-start(bf16[256,1280]{1,0:T(8,128)(2,1)S(1)} %convolution_convert_fusion), channel_id=1, source_target_pairs={{1,0},{2,1},{3,2},{4,3},{5,4},{6,5},{7,6},{8,7},{9,8},{10,9},{11,1... | collective-permute-start | bytes 1966088 | tf_op jit(solution)/shard_map/ppermute | solution.py:10
  6.9 0.7 slice.18
  7.6 0.7 slice.19
  8.3 1.4 fusion.13
  9.8 4.4 %sort.17 = (s32[768]{0:T(1024)}, s32[768]{0:T(1024)S(1)}) sort(s32[768]{0:T(1024)S(1)} %sub.17, s32[768]{0:T(1024)S(1)} %iota.18), dimensions={0}, to_apply=%region_1.2 | sort | flops 7680 | bytes 12288 | tf_op jit(solution)/shard_map/jit(argsort)/sort | solution.py:66
  14.2 1.2 dynamic-slice
  15.4 10.2 %fusion.1 = f32[11,256,1280]{2,1,0:T(8,128)} fusion(bf16[12,256,1280]{2,1,0:T(8,128)(2,1)} %param.7, s32[11,256]{1,0:T(8,128)S(1)} %slice.19, s32[11,256]{1,0:T(8,128)S(1)} %slice.18), kind=kOutput, calls=%fused_computation.7 | convolution fusion | flops 1847656448 | bytes 21649408 | tf_op jit(solution)/shard_map/fst,ftc->fsc/dot_general | solution.py:29
  25.7 1.4 dynamic-update-slice
  27.1 0.7 iota_compare_fusion.3
  27.8 11.3 %all-reduce.2 = s32[16]{0:T(128)S(1)} all-reduce(s32[16]{0:T(128)S(1)} %dynamic-update-slice), channel_id=1, replica_groups=mesh['groups'=2,'seq'=16] {'seq'}, use_global_device_ids=true, to_apply=%add.2 | all-reduce | flops 16 | bytes 128
  39.0 21.6 %while.13 = (s32[]{:T(128)}, s32[]{:T(128)}, s32[]{:T(128)}, s32[16]{0:T(128)S(1)}, s32[]{:T(128)}) while((s32[]{:T(128)}, s32[]{:T(128)}, s32[]{:T(128)}, s32[16]{0:T(128)S(1)}, s32[]{:T(128)}) %tuple.30), condition=%wide.region_6.7_spmd, body=%wide.region_5.6_spmd.sunk | while | flops 5 | bytes 107 | solution.py:23
  41.8 0.7 dynamic_slice.23
  47.2 0.7 dynamic_slice.23
  51.2 0.7 dynamic_slice.23
  61.4 10.6 %multiply_reduce_fusion = f32[12,256]{1,0:T(8,128)S(1)} fusion(f32[12,256]{1,0:T(8,128)S(1)} %maximum_add_fusion.1, f32[1,256,1280]{2,1,0:T(8,128)S(1)} %bitcast_convert_fusion, f32[11,256,1280]{2,1,0:T(8,128)} %fusion.1, bf16[12,256,1280]{2,1,0:T(8,128)(2,1)} %param.7, f32[12,256]{1,0:T(8,128)S(1)} %convert_element_type.36), kind=kLoop, calls=%fused_computation.5 | loop fusion | flops 27522048 | bytes 23629824 | tf_op jit(solution)/shard_map/reduce_sum | solution.py:59
  72.1 0.9 copy-done
  73.0 2.2 %copy-done.1 = bf16[12,256,1280]{2,1,0:T(8,128)(2,1)S(1)} copy-done((bf16[12,256,1280]{2,1,0:T(8,128)(2,1)S(1)}, bf16[12,256,1280]{2,1,0:T(8,128)(2,1)}, u32[]{:S(2)}) %copy-start.1) | copy-done | bytes 7864344
  75.2 5.5 %multiply_convert_fusion = bf16[12,256,1280]{2,1,0:T(8,128)(2,1)} fusion(f32[1280]{0:T(1024)S(1)} %copy-done.4, f32[12,256]{1,0:T(8,128)S(1)} %add_rsqrt_fusion, f32[12,256]{1,0:T(8,128)S(1)} %maximum_add_fusion.1, f32[1,256,1280]{2,1,0:T(8,128)S(1)} %bitcast_convert_fusion, f32[11,256,1280]{2,1,0:T(8,128)S(1)} %copy-done, ...), kind=kLoop, calls=%fused_computation.4 | loop fusion | flops 31457280 | bytes 31499264 | tf_op jit(solution)/shard_map/convert_element_type | solution.py:60
  80.7 12.6 %reshape.126 = bf16[768,5120]{1,0:T(8,128)(2,1)} reshape(bf16[12,256,1280]{2,1,0:T(8,128)(2,1)} %multiply_convert_fusion) | data formatting | bytes 15728640 | tf_op jit(solution)/shard_map/reshape | solution.py:61
  93.3 18.9 %gather_fusion = bf16[768,5120]{1,0:T(8,128)(2,1)} fusion(bf16[768,5120]{1,0:T(8,128)(2,1)} %reshape.126, s32[1024]{0:T(1024)S(1)} %pad_clamp_fusion), kind=kCustom, calls=%fused_computation | custom fusion | bytes 15731712 | tf_op jit(solution)/shard_map/jit(_take)/gather | solution.py:67
  112.2 4.2 %select_select_fusion = bf16[768,5120]{1,0:T(8,128)(2,1)S(1)} fusion(bf16[768,5120]{1,0:T(8,128)(2,1)} %gather_fusion, pred[768]{0:T(1024)(128)(4,1)S(1)} %compare_and_fusion, pred[768]{0:T(1024)(128)(4,1)S(1)} %iota_compare_fusion.3), kind=kLoop, calls=%fused_computation.6 | loop fusion | flops 7864320 | bytes 15730176 | tf_op jit(solution)/shard_map/jit(_where)/select_n | solution.py:69
  116.9 2.1 %pad_maximum_fusion = bf16[1536,5120]{1,0:T(8,128)(2,1)S(1)} fusion(bf16[384,5120]{1,0:T(8,128)(2,1)S(1)} %broadcast_in_dim.80, bf16[768,5120]{1,0:T(8,128)(2,1)S(1)} %select_select_fusion), kind=kLoop, calls=%fused_computation.3 | loop fusion | flops 47185920 | bytes 27525120 | tf_op jit(solution)/shard_map/concatenate | solution.py:71
  119.0 5.5 %copy-done.2 = bf16[1536,5120]{1,0:T(8,128)(2,1)} copy-done((bf16[1536,5120]{1,0:T(8,128)(2,1)}, bf16[1536,5120]{1,0:T(8,128)(2,1)S(1)}, u32[]{:S(2)}) %copy-start.2) | copy-done | bytes 15728664
  124.5 2.2 %constant_dynamic-slice_fusion.1 = (bf16[180,5120]{1,0:T(8,128)(2,1)}, bf16[180,5120]{1,0:T(8,128)(2,1)S(1)}) fusion(bf16[1536,5120]{1,0:T(8,128)(2,1)S(1)} %pad_maximum_fusion, s32[]{:T(128)S(6)} %select_n.63, s32[]{:T(128)S(6)} %select_n.64), kind=kLoop, calls=%fused_computation.36 | loop fusion | bytes 7372808 | tf_op jit(solution)/shard_map/dynamic_slice | solution.py:73
  126.8 6.0 %collective-permute-start.2 = (bf16[180,5120]{1,0:T(8,128)(2,1)}, bf16[180,5120]{1,0:T(8,128)(2,1)}, u32[]{:S(2)}, u32[]{:S(2)}) collective-permute-start(bf16[180,5120]{1,0:T(8,128)(2,1)} %get-tuple-element.95), channel_id=1, source_target_pairs={{0,1},{1,2},{2,3},{3,4},{4,5},{5,6},{6,7},{7,8},{8,9},{9,10},{10,1... | collective-permute-start | bytes 5529608 | tf_op jit(solution)/shard_map/ppermute | solution.py:10
  132.8 1.9 %collective-permute-start.3 = (bf16[180,5120]{1,0:T(8,128)(2,1)S(1)}, bf16[180,5120]{1,0:T(8,128)(2,1)}, u32[]{:S(2)}, u32[]{:S(2)}) collective-permute-start(bf16[180,5120]{1,0:T(8,128)(2,1)S(1)} %get-tuple-element.96), channel_id=1, source_target_pairs={{1,0},{2,1},{3,2},{4,3},{5,4},{6,5},{7,6},{8,7},{9,8},{10,9},{11,1... | collective-permute-start | bytes 5529608 | tf_op jit(solution)/shard_map/ppermute | solution.py:10
  134.7 39.2 %collective-permute-done.2 = bf16[180,5120]{1,0:T(8,128)(2,1)} collective-permute-done((bf16[180,5120]{1,0:T(8,128)(2,1)}, bf16[180,5120]{1,0:T(8,128)(2,1)}, u32[]{:S(2)}, u32[]{:S(2)}) %collective-permute-start.2) | collective-permute-done | bytes 1843232 | tf_op jit(solution)/shard_map/ppermute | solution.py:10
  173.9 5.5 %pad_add_fusion = bf16[384,5120]{1,0:T(8,128)(2,1)} fusion(bf16[180,5120]{1,0:T(8,128)(2,1)} %collective-permute-done.3, bf16[180,5120]{1,0:T(8,128)(2,1)} %collective-permute-done.2, bf16[1536,5120]{1,0:T(8,128)(2,1)} %copy-done.2, s32[]{:T(128)S(6)} %select_n.62), kind=kLoop, calls=%fused_computation.9 | loop fusion | flops 11796480 | bytes 11550724 | tf_op jit(solution)/shard_map/add | solution.py:79
  (39 shorter events, 9.8 us)
Async XLA Ops:
  1.5 59.7 %collective-permute-start.1 = (bf16[256]{0:T(256)(128)(2,1)S(1)}, bf16[256]{0:T(256)(128)(2,1)S(1)}, u32[]{:S(2)}, u32[]{:S(2)}) collective-permute-start(bf16[256]{0:T(256)(128)(2,1)S(1)} %convert_convert_fusion), channel_id=1, source_target_pairs={{1,0},{2,1},{3,2},{4,3},{5,4},{6,5},{7,6},{8,7},{9,8},{10,9},{11,1... | collective-permute-start | bytes 1544 | tf_op jit(solution)/shard_map/ppermute | solution.py:10
  4.9 56.4 %collective-permute-start = (bf16[256,1280]{1,0:T(8,128)(2,1)S(1)}, bf16[256,1280]{1,0:T(8,128)(2,1)S(1)}, u32[]{:S(2)}, u32[]{:S(2)}) collective-permute-start(bf16[256,1280]{1,0:T(8,128)(2,1)S(1)} %convolution_convert_fusion), channel_id=1, source_target_pairs={{1,0},{2,1},{3,2},{4,3},{5,4},{6,5},{7,6},{8,7},{9,8},{10,9},{11,1... | collective-permute-start | bytes 1966088 | tf_op jit(solution)/shard_map/ppermute | solution.py:10
  15.4 23.6 %copy-start.3 = (s32[12,256]{1,0:T(8,128)S(1)}, s32[12,256]{1,0:T(8,128)}, u32[]{:S(2)}) copy-start(s32[12,256]{1,0:T(8,128)} %param.9) | copy-start | bytes 36868
  61.4 11.6 %copy-start = (f32[11,256,1280]{2,1,0:T(8,128)S(1)}, f32[11,256,1280]{2,1,0:T(8,128)}, u32[]{:S(2)}) copy-start(f32[11,256,1280]{2,1,0:T(8,128)} %fusion.1) | copy-start | bytes 43253764
  61.4 13.8 %copy-start.1 = (bf16[12,256,1280]{2,1,0:T(8,128)(2,1)S(1)}, bf16[12,256,1280]{2,1,0:T(8,128)(2,1)}, u32[]{:S(2)}) copy-start(bf16[12,256,1280]{2,1,0:T(8,128)(2,1)} %param.7) | copy-start | bytes 23592964
  61.4 13.8 %copy-start.4 = (f32[1280]{0:T(1024)S(1)}, f32[1280]{0:T(1024)}, u32[]{:S(2)}) copy-start(f32[1280]{0:T(1024)} %param.11) | copy-start | bytes 15364
  119.0 5.5 %copy-start.2 = (bf16[1536,5120]{1,0:T(8,128)(2,1)}, bf16[1536,5120]{1,0:T(8,128)(2,1)S(1)}, u32[]{:S(2)}) copy-start(bf16[1536,5120]{1,0:T(8,128)(2,1)S(1)} %pad_maximum_fusion) | copy-start | bytes 47185924
  126.8 47.2 %collective-permute-start.2 = (bf16[180,5120]{1,0:T(8,128)(2,1)}, bf16[180,5120]{1,0:T(8,128)(2,1)}, u32[]{:S(2)}, u32[]{:S(2)}) collective-permute-start(bf16[180,5120]{1,0:T(8,128)(2,1)} %get-tuple-element.95), channel_id=1, source_target_pairs={{0,1},{1,2},{2,3},{3,4},{4,5},{5,6},{6,7},{7,8},{8,9},{9,10},{10,1... | collective-permute-start | bytes 5529608 | tf_op jit(solution)/shard_map/ppermute | solution.py:10
  132.8 41.2 %collective-permute-start.3 = (bf16[180,5120]{1,0:T(8,128)(2,1)S(1)}, bf16[180,5120]{1,0:T(8,128)(2,1)}, u32[]{:S(2)}, u32[]{:S(2)}) collective-permute-start(bf16[180,5120]{1,0:T(8,128)(2,1)S(1)} %get-tuple-element.96), channel_id=1, source_target_pairs={{1,0},{2,1},{3,2},{4,3},{5,4},{6,5},{7,6},{8,7},{9,8},{10,9},{11,1... | collective-permute-start | bytes 5529608 | tf_op jit(solution)/shard_map/ppermute | solution.py:10
where the time goes:
time: 180 us; the launch traced here: 179 us
  local copies, waits for them, and re-layouts  58.8 us (33%)
  waiting for transfers between devices  39.2 us (22%)
  other arithmetic  35.2 us (20%)
  starting transfers between devices  11.8 us (7%)
  matrix products  11.7 us (6%)
  blocking collectives  11.3 us (6%)
  loops' own time  11.2 us (6%)
    ppermute x4, waiting for transfers between devices, shifted(): lax.ppermute(value, axis, [(source, source + steps) for source in range(l...  39.2 us
    gather x1, local copies, waits for them, and re-layouts, body(): compact = jnp.take(group_rows, kept_order, axis=0)  18.9 us
    reshape x1, local copies, waits for them, and re-layouts, body(): group_rows = normed.reshape(count_frames * groups, 4 * width)  12.6 us
    ppermute x4, starting transfers between devices, shifted(): lax.ppermute(value, axis, [(source, source + steps) for source in range(l...  11.8 us
    dot_general x2, matrix products, absorb(): jnp.einsum('fst,ftc->fsc', weighted.astype(jnp.bfloat16), source, preferr...  11.7 us
    unnamed x13, local copies, waits for them, and re-layouts  11.3 us
    unnamed x1, blocking collectives  11.3 us
    another operation x1, loops' own time, entering(): return lax.fori_loop(0, length, turn, start)  11.2 us
  transfers between devices with their start and end apart: 4, of which 1 were waited for; matrix products, arithmetic and copies ran while one was open for 19% of the time, Pallas kernels for 0%

commit v1 on v0

v1 whole, which is shorter than its diff:
```python
import functools

import jax
import jax.numpy as jnp
from jax import lax
from jax.experimental import pallas as pl
from jax.experimental.pallas import tpu as pltpu
from jax.sharding import PartitionSpec as P

TILE = 16


def exchange_kernel(n, keep_ref, match_ref, weight_ref, all_ref, own, send_sem, recv_sem):
    me = lax.axis_index("seq")
    barrier = pltpu.get_barrier_semaphore()

    def greet(step, carry):
        peer = lax.rem(me + step, n)
        pl.semaphore_signal(
            barrier, inc=1, device_id={"seq": peer}, device_id_type=pl.DeviceIdType.MESH
        )
        return carry

    lax.fori_loop(1, n, greet, 0)
    count = jnp.sum(keep_ref[...].astype(jnp.float32), keepdims=True).astype(jnp.int32)
    own[0:1, :] = match_ref[0:1, :]
    own[1:2, :] = weight_ref[0:1, :]
    own[2:8, :] = jnp.broadcast_to(count, (6, own.shape[1]))
    all_ref[pl.ds(me, 1)] = own[...][None]
    pl.semaphore_wait(barrier, n - 1)

    def copy(step):
        peer = lax.rem(me + step, n)
        return pltpu.make_async_remote_copy(
            src_ref=own,
            dst_ref=all_ref.at[me],
            send_sem=send_sem.at[step],
            recv_sem=recv_sem.at[step],
            device_id={"seq": peer},
            device_id_type=pl.DeviceIdType.MESH,
        )

    def send(step, carry):
        copy(step).start()
        return carry

    def finish(step, carry):
        copy(step).wait()
        return carry

    lax.fori_loop(1, n, send, 0)
    lax.fori_loop(1, n, finish, 0)


def exchange(keep, match, weight):
    n = lax.axis_size("seq")
    tokens = match.shape[1]
    return pl.pallas_call(
        functools.partial(exchange_kernel, n),
        out_shape=jax.ShapeDtypeStruct((n, 8, tokens), jnp.int32),
        in_specs=[pl.BlockSpec(memory_space=pltpu.VMEM)] * 3,
        out_specs=pl.BlockSpec(memory_space=pltpu.VMEM),
        scratch_shapes=[
            pltpu.VMEM((8, tokens), jnp.int32),
            pltpu.SemaphoreType.DMA((n,)),
            pltpu.SemaphoreType.DMA((n,)),
        ],
        compiler_params=pltpu.CompilerParams(collective_id=0, has_side_effects=True),
    )(keep, match, weight)


def merge_kernel(
    side,
    starts,
    keep_ref,
    match_ref,
    weight_ref,
    next_ref,
    gain_ref,
    frame_ref,
    after_ref,
    first_ref,
    back_ref,
    own_ref,
    ahead_ref,
    window,
    own_key,
    inc_key,
    inc_weight,
    sems,
):
    count, groups = keep_ref.shape
    tokens = match_ref.shape[1]
    per = tokens // groups
    width = gain_ref.shape[1]
    rows = groups + TILE
    kept_dev = own_ref.shape[0]
    f = pl.program_id(0)

    @pl.when(f == 0)
    def _():
        keep = keep_ref[...].astype(jnp.bfloat16)
        g = lax.broadcasted_iota(jnp.int32, (groups, tokens), 0)
        t_group = lax.broadcasted_iota(jnp.int32, (groups, tokens), 1) // per
        below = (g < t_group).astype(jnp.bfloat16)
        same = (g == t_group).astype(jnp.bfloat16)
        before = jnp.dot(keep, below, preferred_element_type=jnp.float32)
        kept = jnp.dot(keep, same, preferred_element_type=jnp.float32)
        token = lax.broadcasted_iota(jnp.int32, (count, tokens), 1)
        own_key[0:count, :] = jnp.where(
            kept > 0.5, (token % per) * rows + before.astype(jnp.int32), -1000
        )
        at = lax.broadcasted_iota(jnp.int32, (groups, groups), 0)
        other = lax.broadcasted_iota(jnp.int32, (groups, groups), 1)
        column = lax.dot_general(
            (other < at).astype(jnp.bfloat16),
            keep,
            (((1,), (1,)), ((), ())),
            preferred_element_type=jnp.float32,
        )
        for k in range(count):
            if k + 1 < count:
                target = match_ref[k + 1 : k + 2, :]
                inc_weight[k : k + 1, :] = weight_ref[k + 1 : k + 2, :]
            else:
                target = next_ref[0:1, :]
                inc_weight[k : k + 1, :] = next_ref[1:2, :]
            place = jnp.sum(
                jnp.where(g == target // per, column[:, k : k + 1], 0.0), axis=0, keepdims=True
            )
            inc_key[k : k + 1, :] = jnp.where(
                target >= 0, (target % per) * rows + place.astype(jnp.int32), -1000
            )

    start = starts[f]
    base = pl.multiple_of((start // TILE) * TILE, TILE)
    off = start - base

    def work(later_ref):
        line = lax.broadcasted_iota(jnp.int32, (per * rows, tokens), 0) - off
        mine = jnp.where(
            line == own_key[pl.ds(f, 1), :], weight_ref[pl.ds(f, 1), :].astype(jnp.float32), 0.0
        )
        theirs = jnp.where(
            line == inc_key[pl.ds(f, 1), :], inc_weight[pl.ds(f, 1), :].astype(jnp.float32), 0.0
        )
        total = jnp.maximum(jnp.sum(mine + theirs, axis=1, keepdims=True), 1.0)
        summed = jnp.dot(
            mine.astype(jnp.bfloat16), frame_ref[0], preferred_element_type=jnp.float32
        ) + jnp.dot(theirs.astype(jnp.bfloat16), later_ref[0], preferred_element_type=jnp.float32)
        mean = jnp.sum(summed * summed, axis=1, keepdims=True) * (1.0 / width)
        scale = lax.rsqrt(mean + 1e-06 * total * total)
        normed = summed * scale * gain_ref[...]
        old_rows = lax.broadcasted_iota(jnp.int32, (TILE, width), 0) < off
        for j in range(per):
            cols = slice(j * width, (j + 1) * width)
            old = window[pl.ds(base, TILE), cols].astype(jnp.float32)
            head = jnp.where(old_rows, old, normed[j * rows : j * rows + TILE])
            window[pl.ds(base, TILE), cols] = head.astype(jnp.bfloat16)
            window[pl.ds(pl.multiple_of(base + TILE, TILE), groups), cols] = normed[
                j * rows + TILE : (j + 1) * rows
            ].astype(jnp.bfloat16)

    @pl.when(f < count - 1)
    def _():
        work(after_ref)

    @pl.when(f == count - 1)
    def _():
        work(first_ref)
        copies = [
            pltpu.make_async_copy(window.at[pl.ds(0, side)], back_ref, sems.at[0]),
            pltpu.make_async_copy(window.at[pl.ds(side + kept_dev, side)], ahead_ref, sems.at[1]),
            pltpu.make_async_copy(window.at[pl.ds(side, kept_dev)], own_ref, sems.at[2]),
        ]
        for copy in copies:
            copy.start()
        for copy in copies:
            copy.wait()


def merge(starts, keep, match, weight, after, gain, frames, first, side, kept_dev):
    count, tokens, width = frames.shape
    groups = keep.shape[1]
    row = tokens // groups * width
    whole = pl.BlockSpec(memory_space=pltpu.VMEM)
    return pl.pallas_call(
        functools.partial(merge_kernel, side),
        out_shape=[
            jax.ShapeDtypeStruct((side, row), jnp.bfloat16),
            jax.ShapeDtypeStruct((kept_dev, row), jnp.bfloat16),
            jax.ShapeDtypeStruct((side, row), jnp.bfloat16),
        ],
        grid_spec=pltpu.PrefetchScalarGridSpec(
            num_scalar_prefetch=1,
            grid=(count,),
            in_specs=[
                whole,
                whole,
                whole,
                whole,
                whole,
                pl.BlockSpec((1, tokens, width), lambda f, s: (f, 0, 0)),
                pl.BlockSpec((1, tokens, width), lambda f, s: (jnp.minimum(f + 1, count - 1), 0, 0)),
                pl.BlockSpec((1, tokens, width), lambda f, s: (0, 0, 0)),
            ],
            out_specs=[pl.BlockSpec(memory_space=pl.ANY)] * 3,
            scratch_shapes=[
                pltpu.VMEM((2 * side + kept_dev + groups + TILE, row), jnp.bfloat16),
                pltpu.VMEM((count, tokens), jnp.int32),
                pltpu.VMEM((count, tokens), jnp.int32),
                pltpu.VMEM((count, tokens), jnp.int32),
                pltpu.SemaphoreType.DMA((3,)),
            ],
        ),
        compiler_params=pltpu.CompilerParams(vmem_limit_bytes=48 * 1024 * 1024),
    )(starts, keep, match, weight, after, gain, frames, frames, first)


def shifted(value, steps):
    n = lax.axis_size("seq")
    pairs = [(i, i + steps) for i in range(max(0, -steps), min(n, n - steps))]
    return lax.ppermute(value, "seq", pairs)


def body(frames, match, weight, keep, gain):
    count, tokens, width = frames.shape
    groups = keep.shape[1]
    kept_dev = count * groups // 2
    drift = kept_dev // 2 - count
    side = -(-drift // TILE) * TILE
    n = lax.axis_size("seq")
    me = lax.axis_index("seq")
    first = shifted(frames[:1], -1)
    everyone = exchange(keep, match, weight)
    counts = everyone[:, 2, 0]
    device = jnp.arange(n, dtype=jnp.int32)
    drift_here = jnp.sum(jnp.where(device < me, counts - kept_dev, 0))
    drift_next = jnp.sum(jnp.where(device <= me, counts - kept_dev, 0))
    after = lax.dynamic_index_in_dim(everyone, jnp.minimum(me + 1, n - 1), 0, keepdims=False)
    after = jnp.where((me == n - 1) & (jnp.arange(8)[:, None] == 1), 0, after)
    per_frame = jnp.sum(keep, axis=1)
    frame_at = jnp.arange(count, dtype=jnp.int32)
    earlier = jnp.sum(jnp.where(frame_at[None, :] < frame_at[:, None], per_frame[None, :], 0), axis=1)
    starts = earlier + drift_here + side
    back, own, ahead = merge(
        starts, keep, match, weight, after, gain.reshape(1, width), frames, first, side, kept_dev
    )
    from_next = shifted(back, -1)
    from_before = shifted(ahead, 1)
    line = jnp.arange(side, dtype=jnp.int32)[:, None]
    top = jnp.where(line < drift_here, from_before, own[:side])
    bottom = jnp.where(line >= side + drift_next, from_next, own[kept_dev - side :])
    return jnp.concatenate([top, own[side : kept_dev - side], bottom], axis=0)


def solution(mesh):
    placed = (
        P(("groups", "seq"), None, None),
        P(("groups", "seq"), None),
        P(("groups", "seq"), None),
        P(("groups", "seq"), None),
        P(),
    )
    return jax.shard_map(
        body, mesh=mesh, in_specs=placed, out_specs=P(("groups", "seq"), None), check_vma=False
    )
```

time: 180 us -> 97 us (0.54)
  local copies, waits for them, and re-layouts: 58.8 us -> 3.97 us
  Pallas kernels: 0 us -> 32.4 us
  other arithmetic: 35.2 us -> 11.9 us
  matrix products: 11.7 us -> 0 us
  blocking collectives: 11.3 us -> 0 us
  loops' own time: 11.2 us -> 0 us
  starting transfers between devices: 11.8 us -> 7.56 us
    pallas_call x0 -> x2, Pallas kernels: none -> 32.4 us  [the longest x1 17.5 us: merge(): pl.pallas_call(functools.partial(merge_kernel, side), out_shape=[jax.Shap...]
    gather x1 -> x0, local copies, waits for them, and re-layouts: 18.9 us -> none  [body(): compact = jnp.take(group_rows, kept_order, axis=0)]
    dynamic_slice x17 -> x0, local copies, waits for them, and re-layouts: 12.6 us -> none  [the longest x16 10.4 us: turn(): new = combine(before, everything[k])]
    reshape x1, local copies, waits for them, and re-layouts: 12.6 us -> 0.7 us  [body(): gain.reshape(1, width)]
    dot_general x2 -> x0, matrix products: 11.7 us -> none  [absorb(): jnp.einsum('fst,ftc->fsc', weighted.astype(jnp.bfloat16), source, preferr...]
    unnamed x1 -> x0, blocking collectives: 11.3 us -> none
    another operation x1 -> x0, loops' own time: 11.2 us -> none  [entering(): return lax.fori_loop(0, length, turn, start)]
    reduce_sum x4 -> x3, other arithmetic: 12.7 us -> 1.6 us  [the longest x1 0.81 us: body(): per_frame = jnp.sum(keep, axis=1)]
  transfers between devices with their start and end apart: 4 -> 3, of which waited for: 1 -> 1; matrix products, arithmetic and copies ran while one was open for 19% -> 6% of each run, Pallas kernels for 0% -> 16%
where the time goes in v1:
time: 97 us; the launch traced here: 96.1 us
  waiting for transfers between devices  39.7 us (41%)
  Pallas kernels  32.4 us (33%)
  other arithmetic  11.9 us (12%)
  starting transfers between devices  7.56 us (8%)
  local copies, waits for them, and re-layouts  3.97 us (4%)
    ppermute x3, waiting for transfers between devices, shifted(): return lax.ppermute(value, 'seq', pairs)  39.7 us
    pallas_call x1, Pallas kernels, merge(): pl.pallas_call(functools.partial(merge_kernel, side), out_shape=[jax.Shap...  17.5 us
    pallas_call x1, Pallas kernels, exchange(): pl.pallas_call(functools.partial(exchange_kernel, n), out_shape=jax.Shape...  14.9 us
    ppermute x3, starting transfers between devices, shifted(): return lax.ppermute(value, 'seq', pairs)  7.56 us
    select_n x2, other arithmetic, body(): top = jnp.where(line < drift_here, from_before, own[:side])  7 us
    unnamed x6, local copies, waits for them, and re-layouts  2.13 us
  transfers between devices with their start and end apart: 3, of which 1 were waited for; matrix products, arithmetic and copies ran while one was open for 6% of the time, Pallas kernels for 16%

profile of v1, /device:TPU:1, one launch (start us, length us, event | category | flops | bytes accessed | tf_op | source)
XLA Modules:
  0.0 96.1 jit_solution(13450336598222356470)
XLA Ops:
  0.0 1.1 %slice.13 = bf16[1,256,1280]{2,1,0:T(8,128)(2,1)S(1)} slice(bf16[12,256,1280]{2,1,0:T(8,128)(2,1)} %after_ref.1), slice={[0:1], [0:256], [0:1280]} | slice | bytes 1310720 | tf_op jit(solution)/shard_map/slice | solution.py:234
  1.1 2.0 %collective-permute-start = (bf16[1,256,1280]{2,1,0:T(8,128)(2,1)S(1)}, bf16[1,256,1280]{2,1,0:T(8,128)(2,1)S(1)}, u32[]{:S(2)}, u32[]{:S(2)}) collective-permute-start(bf16[1,256,1280]{2,1,0:T(8,128)(2,1)S(1)} %slice.13), channel_id=1, source_target_pairs={{1,0},{2,1},{3,2},{4,3},{5,4},{6,5},{7,6},{8,7},{9,8},{10,9},{11,1... | collective-permute-start | bytes 1966088 | tf_op jit(solution)/shard_map/ppermute | solution.py:223
  3.1 0.8 reduce_sum.37
  3.9 0.1 select_reduce_fusion
  4.0 0.7 reshape.23.gain_ref
  4.8 14.9 %shard_map.55 = s32[16,8,256]{2,1,0:T(8,128)} custom-call(s32[12,64]{1,0:T(8,128)} %keep_ref.3, s32[12,256]{1,0:T(8,128)} %match_ref.3, s32[12,256]{1,0:T(8,128)} %weight_ref.3), custom_call_target="tpu_custom_call" | custom-call | tf_op jit(solution)/shard_map/pallas_call | solution.py:58
  19.7 1.2 %add_reduce_fusion = s32[16]{0:T(128)S(1)} fusion(s32[16,8,256]{2,1,0:T(8,128)} %shard_map.55), kind=kLoop, calls=%fused_computation.6 | loop fusion | flops 16 | bytes 128 | tf_op jit(solution)/shard_map/sub | solution.py:238
  20.9 0.7 fusion.1
  21.6 0.6 add_add_fusion.starts
  22.2 0.8 bitcast_select_fusion.next_ref
  23.0 0.0 collective-permute-done.first_ref
  23.0 0.0 copy-start
  23.0 0.7 copy-done
  23.7 0.0 copy-start.1
  23.7 0.7 copy-done.1
  24.4 0.0 copy-start.2
  24.4 0.7 copy-done.2
  25.1 17.5 %shard_map.56 = (bf16[192,5120]{1,0:T(8,128)(2,1)S(1)}, bf16[384,5120]{1,0:T(8,128)(2,1)}, bf16[192,5120]{1,0:T(8,128)(2,1)}) custom-call(s32[12]{0:T(128)S(1)} %add_add_fusion.starts, s32[12,64]{1,0:T(8,128)S(1)} %copy-done, s32[12,256]{1,0:T(8,128)S(1)} %copy-done.1, s32[12,256]{1,0:T(8,128)S(1)} %copy-done.2, s32[8,256]{1,0:T(8,128)S(1)} %bitcast_select_fusion.next_ref, ...), custom_call_target="tpu_custom_call" | custom-call | tf_op jit(solution)/shard_map/pallas_call | solution.py:187
  42.6 3.5 %collective-permute-start.1 = (bf16[192,5120]{1,0:T(8,128)(2,1)}, bf16[192,5120]{1,0:T(8,128)(2,1)}, u32[]{:S(2)}, u32[]{:S(2)}) collective-permute-start(bf16[192,5120]{1,0:T(8,128)(2,1)} %get-tuple-element.8), channel_id=1, source_target_pairs={{0,1},{1,2},{2,3},{3,4},{4,5},{5,6},{6,7},{7,8},{8,9},{9,10},{10,1... | collective-permute-start | bytes 5898248 | tf_op jit(solution)/shard_map/ppermute | solution.py:223
  46.2 2.0 %collective-permute-start.2 = (bf16[192,5120]{1,0:T(8,128)(2,1)S(1)}, bf16[192,5120]{1,0:T(8,128)(2,1)}, u32[]{:S(2)}, u32[]{:S(2)}) collective-permute-start(bf16[192,5120]{1,0:T(8,128)(2,1)S(1)} %get-tuple-element.10), channel_id=1, source_target_pairs={{1,0},{2,1},{3,2},{4,3},{5,4},{6,5},{7,6},{8,7},{9,8},{10,9},{11,1... | collective-permute-start | bytes 5898248 | tf_op jit(solution)/shard_map/ppermute | solution.py:223
  48.8 0.6 iota_compare_fusion.1
  49.5 39.6 %collective-permute-done.1 = bf16[192,5120]{1,0:T(8,128)(2,1)} collective-permute-done((bf16[192,5120]{1,0:T(8,128)(2,1)}, bf16[192,5120]{1,0:T(8,128)(2,1)}, u32[]{:S(2)}, u32[]{:S(2)}) %collective-permute-start.1) | collective-permute-done | bytes 1966112 | tf_op jit(solution)/shard_map/ppermute | solution.py:223
  89.1 0.0 collective-permute-done.2
  89.1 7.0 %slice_select_fusion.1 = (bf16[384,5120]{1,0:T(8,128)(2,1)}, bf16[384,5120]{1,0:T(8,128)(2,1)}) fusion(bf16[192,5120]{1,0:T(8,128)(2,1)} %collective-permute-done.1, bf16[384,5120]{1,0:T(8,128)(2,1)} %get-tuple-element.9, pred[192]{0:T(512)(128)(4,1)S(1)} %get-tuple-element.16, ...), kind=kLoop, output_to_operand_aliasing={{0}: (5, {}), {1}: (5, {})}, calls=%fused_computation.2 | loop fusion | flops 1966080 | bytes 11796864 | tf_op jit(solution)/shard_map/jit(_where)/select_n | solution.py:252
  (2 shorter events, 0.0 us)
Async XLA Ops:
  1.1 21.9 %collective-permute-start = (bf16[1,256,1280]{2,1,0:T(8,128)(2,1)S(1)}, bf16[1,256,1280]{2,1,0:T(8,128)(2,1)S(1)}, u32[]{:S(2)}, u32[]{:S(2)}) collective-permute-start(bf16[1,256,1280]{2,1,0:T(8,128)(2,1)S(1)} %slice.13), channel_id=1, source_target_pairs={{1,0},{2,1},{3,2},{4,3},{5,4},{6,5},{7,6},{8,7},{9,8},{10,9},{11,1... | collective-permute-start | bytes 1966088 | tf_op jit(solution)/shard_map/ppermute | solution.py:223
  23.0 0.7 copy-start
  23.7 0.7 copy-start.1
  24.4 0.7 copy-start.2
  42.6 46.5 %collective-permute-start.1 = (bf16[192,5120]{1,0:T(8,128)(2,1)}, bf16[192,5120]{1,0:T(8,128)(2,1)}, u32[]{:S(2)}, u32[]{:S(2)}) collective-permute-start(bf16[192,5120]{1,0:T(8,128)(2,1)} %get-tuple-element.8), channel_id=1, source_target_pairs={{0,1},{1,2},{2,3},{3,4},{4,5},{5,6},{6,7},{7,8},{8,9},{9,10},{10,1... | collective-permute-start | bytes 5898248 | tf_op jit(solution)/shard_map/ppermute | solution.py:223
  46.2 42.9 %collective-permute-start.2 = (bf16[192,5120]{1,0:T(8,128)(2,1)S(1)}, bf16[192,5120]{1,0:T(8,128)(2,1)}, u32[]{:S(2)}, u32[]{:S(2)}) collective-permute-start(bf16[192,5120]{1,0:T(8,128)(2,1)S(1)} %get-tuple-element.10), channel_id=1, source_target_pairs={{1,0},{2,1},{3,2},{4,3},{5,4},{6,5},{7,6},{8,7},{9,8},{10,9},{11,1... | collective-permute-start | bytes 5898248 | tf_op jit(solution)/shard_map/ppermute | solution.py:223
